TPU v7x, 32 devices: a whole 2x2x4 slice. The times are simulated.
32 devices in a mesh: group: 2 (over y), row: 16 (over z, x, core).
Axes of the slice: x: 2, y: 2, z: 4, core: 2. Of those that a mesh axis runs over, the one named last changes fastest.
Arguments:
- x_first: bfloat16 [16384, 384], P('row', 'group'), parts along dimension 1, may hold values from -6 to 6
- x_layer: bfloat16 [24576, 384], P('row', 'group'), parts along dimension 1, may hold values from -6 to 6
- upstream: bfloat16 [16384, 384], P('row', 'group'), parts along dimension 1, may hold values from -4 to 4
- weight: bfloat16 [16384, 24576], P('row'), may hold values from -0.0546875 to 0.0546875
- bias: float32 [16384], P('row'), may hold values from -6 to 6
Outputs:
- first_grad: bfloat16 [16384, 384], P('row', 'group'), parts along dimension 1
- layer_grad: bfloat16 [24576, 384], P('row', 'group'), parts along dimension 1
- weight_grad: bfloat16 [32768, 24576], P(('group', 'row')), parts along dimension 0
- bias_grad: float32 [32768], P(('group', 'row')), parts along dimension 0
There are 2 independent parts, one for each index of `group`. A program takes and returns all parts, laid end to end along the dimension named above; an argument that names none is the same for every part. Nothing has to cross between parts.
All inputs are finite; a program needn't handle non-finite values.
Results may differ from a plain program's by a relative error of at most 0.005.
Values may be sent and summed in bfloat16 or wider, within the bound.
A program may use at most 256 MiB of HBM per device.

v0:
```python
import jax
import jax.numpy as jnp
from jax import lax
from jax.sharding import PartitionSpec as P


def on_device(x_first, x_layer, upstream, weight, bias):
    gathered = lax.all_gather(x_layer, "row", axis=0, tiled=True)
    affine = jnp.dot(weight, gathered, preferred_element_type=jnp.float32) + bias[:, None]
    upstream_wide = upstream.astype(jnp.float32)
    first_grad = (upstream_wide * affine).astype(jnp.bfloat16)
    modulated = (upstream_wide * x_first.astype(jnp.float32)).astype(jnp.bfloat16)
    weight_grad = lax.dot_general(
        modulated, gathered, (((1,), (1,)), ((), ())), preferred_element_type=jnp.float32
    ).astype(jnp.bfloat16)
    bias_grad = jnp.sum(modulated.astype(jnp.float32), axis=1)
    layer_grad = lax.psum_scatter(
        lax.dot_general(
            weight, modulated, (((0,), (0,)), ((), ())), preferred_element_type=jnp.float32
        ),
        "row",
        scatter_dimension=0,
        tiled=True,
    ).astype(jnp.bfloat16)
    return (first_grad, layer_grad, weight_grad, bias_grad)


def solution(mesh):
    in_specs = (P("row", "group"), P("row", "group"), P("row", "group"), P("row", None), P("row"))
    out_specs = (
        P("row", "group"),
        P("row", "group"),
        P(("group", "row"), None),
        P(("group", "row")),
    )
    return jax.shard_map(
        on_device, mesh=mesh, in_specs=in_specs, out_specs=out_specs, check_vma=False
    )
```

profile of v0, /device:TPU:0, one launch (start us, length us, event | category | flops | bytes accessed | tf_op | source)
XLA Modules:
  0.0 300.7 jit_solution(10873437468651281367)
XLA Ops:
  7.2 0.0 copy-start.1
  7.2 0.0 copy-start
  7.2 0.0 all-gather.2.cloned.1.call-start
  7.2 0.7 all-gather.2.cloned.1.call-update
  7.9 0.0 reduce-scatter.2.cloned.1.call-start
  8.0 30.6 %convolution_bitcast_fusion = f32[24576,192]{0,1:T(8,128)} fusion(bf16[1024,24576]{1,0:T(8,128)(2,1)} %param.8, bf16[1024,192]{0,1:T(8,128)(2,1)} %param.7, bf16[1024,192]{0,1:T(8,128)(2,1)} %param.5), kind=kOutput, calls=%fused_computation.1 | convolution fusion | flops 9664462848 | bytes 69992448 | tf_op jit(solution)/shard_map/dot_general | solution.py:18
  38.5 0.0 copy-start.2
  38.5 0.0 reduce-scatter.2.cloned.1.call-update
  38.6 0.0 copy-done.1
  38.6 0.0 copy-done
  38.6 0.7 convert_reduce_fusion
  39.3 55.2 %all-gather.2.cloned.1.call-done = bf16[24576,192]{0,1:T(8,128)(2,1)} async-done(((bf16[1536,192]{0,1:T(8,128)(2,1)}), bf16[24576,192]{0,1:T(8,128)(2,1)}) %all-gather.2.cloned.1.call-update) | async-done | bytes 9437200 | tf_op jit(solution)/shard_map/all_gather | solution.py:8
  94.5 32.5 %convolution_convert_fusion = bf16[1024,24576]{1,0:T(8,128)(2,1)} fusion(bf16[24576,192]{0,1:T(8,128)(2,1)} %all-gather.2.cloned.1.call-done, bf16[1024,192]{0,1:T(8,128)(2,1)S(1)} %copy-done.1, bf16[1024,192]{0,1:T(8,128)(2,1)S(1)} %copy-done), kind=kOutput, calls=%fused_computation | convolution fusion | flops 9689628672 | bytes 60555264 | tf_op jit(solution)/shard_map/dot_general | solution.py:13
  127.0 0.0 copy-done.2
  127.0 25.9 %fusion.1 = bf16[1024,192]{0,1:T(8,128)(2,1)} fusion(bf16[1024,24576]{1,0:T(8,128)(2,1)} %param.8, bf16[24576,192]{0,1:T(8,128)(2,1)} %all-gather.2.cloned.1.call-done, bf16[1024,192]{0,1:T(8,128)(2,1)S(1)} %copy-done.1, f32[1024]{0:T(1024)S(1)} %copy-done.2), kind=kOutput, calls=%fused_computation.4 | convolution fusion | flops 9664462848 | bytes 60559360 | tf_op jit(solution)/shard_map/dot_general | solution.py:9
  152.9 138.8 %reduce-scatter.2.cloned.1.call-done = f32[1536,192]{0,1:T(8,128)} async-done(((f32[24576,192]{0,1:T(8,128)}), f32[1536,192]{0,1:T(8,128)}) %reduce-scatter.2.cloned.1.call-update) | async-done | bytes 1179664 | tf_op jit(solution)/shard_map/reduce_scatter | solution.py:17
  291.7 2.1 convert_element_type.25
Async XLA Ops:
  7.2 31.4 %copy-start.1 = (bf16[1024,192]{0,1:T(8,128)(2,1)S(1)}, bf16[1024,192]{0,1:T(8,128)(2,1)}, u32[]{:S(2)}) copy-start(bf16[1024,192]{0,1:T(8,128)(2,1)} %param.7) | copy-start | bytes 1179652
  7.2 31.4 %copy-start = (bf16[1024,192]{0,1:T(8,128)(2,1)S(1)}, bf16[1024,192]{0,1:T(8,128)(2,1)}, u32[]{:S(2)}) copy-start(bf16[1024,192]{0,1:T(8,128)(2,1)} %param.5) | copy-start | bytes 1179652
  7.2 87.3 %all-gather.2.cloned.1.call-start = ((), (), s32[]{:S(2)}) async-start(), calls=%async_computation.1 | async-start | bytes 10027008 | tf_op jit(solution)/shard_map/all_gather | solution.py:8
  7.9 283.8 %reduce-scatter.2.cloned.1.call-start = ((), (), s32[]{:S(2)}) async-start(), calls=%async_computation.2 | async-start | bytes 20054016 | tf_op jit(solution)/shard_map/reduce_scatter | solution.py:17
  38.5 88.5 %copy-start.2 = (f32[1024]{0:T(1024)S(1)}, f32[1024]{0:T(1024)}, u32[]{:S(2)}) copy-start(f32[1024]{0:T(1024)} %param.9) | copy-start | bytes 12292
Sparse Core Ops, SparseCore 0:
  10.3 84.1 all-gather.1
  98.6 193.0 reduce-scatter.1
where the time goes:
time: 301 us
  waiting for transfers between devices  195 us (65%)
  matrix products  89 us (30%)
  between operations  14.1 us (5%)
    reduce_scatter x1, waiting for transfers between devices, on_device(): lax.psum_scatter(lax.dot_general(weight, modulated, (((0,), (0,)), ((), (...  139 us
    all_gather x1, waiting for transfers between devices, on_device(): gathered = lax.all_gather(x_layer, 'row', axis=0, tiled=True)  55.2 us
    dot_general x1, matrix products, on_device(): lax.dot_general(modulated, gathered, (((1,), (1,)), ((), ())), preferred_...  32.5 us
    dot_general x1, matrix products, on_device(): lax.dot_general(weight, modulated, (((0,), (0,)), ((), ())), preferred_el...  30.6 us
    dot_general x1, matrix products, on_device(): jnp.dot(weight, gathered, preferred_element_type=jnp.float32)  25.9 us
  transfers between devices with their start and end apart: 2, of which 2 were waited for; matrix products, arithmetic and copies ran while one was open for 30% of the time, Pallas kernels for 0%

commit v1 on v0

v1 whole, which is shorter than its diff:
```python
import functools

import jax
import jax.numpy as jnp
from jax import lax
from jax.experimental import pallas as pl
from jax.experimental.pallas import tpu as pltpu
from jax.sharding import PartitionSpec as P

F32 = jnp.float32
BF16 = jnp.bfloat16


def ring_of(n):
    width = {8: 2, 64: 4}.get(n, 2)
    depth = n // width
    walk = []
    for z in range(depth):
        xs = list(range(1, width))
        walk += [z * width + x for x in (xs if z % 2 == 0 else xs[::-1])]
    return walk + [z * width for z in reversed(range(depth))]


def partial_kernel(parts, where, mod_t, w, away, own):
    t = pl.program_id(0)
    out = jnp.dot(mod_t[...], w[...], preferred_element_type=F32)

    @pl.when(t < parts)
    def _():
        away[...] = out.astype(away.dtype)

    @pl.when(t >= parts)
    def _():
        own[...] = out


def partials(where, mod_t, weight, block, parts):
    samples, rows = mod_t.shape
    tile = block // parts
    return pl.pallas_call(
        functools.partial(partial_kernel, parts),
        grid_spec=pltpu.PrefetchScalarGridSpec(
            num_scalar_prefetch=1,
            grid=(2 * parts,),
            in_specs=[
                pl.BlockSpec((samples, rows), lambda t, s: (0, 0)),
                pl.BlockSpec((rows, tile), lambda t, s: (0, jnp.where(t < parts, s[1] * parts + t, s[0] * parts + t - parts))),
            ],
            out_specs=[
                pl.BlockSpec((samples, tile), lambda t, s: (0, jnp.minimum(t, parts - 1))),
                pl.BlockSpec((samples, tile), lambda t, s: (0, jnp.maximum(t - parts, 0))),
            ],
        ),
        out_shape=[jax.ShapeDtypeStruct((samples, block), BF16), jax.ShapeDtypeStruct((samples, block), F32)],
        compiler_params=pltpu.CompilerParams(vmem_limit_bytes=24 << 20),
        cost_estimate=pl.CostEstimate(flops=4 * samples * rows * block, bytes_accessed=4 * rows * block, transcendentals=0),
    )(where, mod_t, weight)


def forward_kernel(parts, where, w, mod, xa, xb, total_in, grad_in, total, grad):
    t = pl.program_id(0)

    @pl.when(t == 0)
    def _():
        total[...] = total_in[...]

    def step(x):
        total[...] += lax.dot_general(w[...], x[...], (((1,), (1,)), ((), ())), preferred_element_type=F32)
        grad[...] = jnp.dot(mod[...], x[...], preferred_element_type=F32).astype(grad.dtype)

    pl.when(t < parts)(lambda: step(xa))
    pl.when(t >= parts)(lambda: step(xb))


def forward(where, weight, mod, xa, xb, total, grad, parts):
    rows, samples = mod.shape
    block = xa.shape[1]
    tile = block // parts

    def column(t, s):
        return (0, jnp.where(t < parts, s[0] * parts + t, s[1] * parts + t - parts))

    return pl.pallas_call(
        functools.partial(forward_kernel, parts),
        grid_spec=pltpu.PrefetchScalarGridSpec(
            num_scalar_prefetch=1,
            grid=(2 * parts,),
            in_specs=[
                pl.BlockSpec((rows, tile), column),
                pl.BlockSpec((rows, samples), lambda t, s: (0, 0)),
                pl.BlockSpec((samples, tile), lambda t, s: (0, jnp.minimum(t, parts - 1))),
                pl.BlockSpec((samples, tile), lambda t, s: (0, jnp.maximum(t - parts, 0))),
                pl.BlockSpec((rows, samples), lambda t, s: (0, 0)),
                pl.BlockSpec(memory_space=pl.ANY),
            ],
            out_specs=[
                pl.BlockSpec((rows, samples), lambda t, s: (0, 0)),
                pl.BlockSpec((rows, tile), column),
            ],
        ),
        out_shape=[jax.ShapeDtypeStruct(total.shape, F32), jax.ShapeDtypeStruct(grad.shape, BF16)],
        input_output_aliases={5: 0, 6: 1},
        compiler_params=pltpu.CompilerParams(vmem_limit_bytes=32 << 20),
        cost_estimate=pl.CostEstimate(flops=8 * samples * rows * block, bytes_accessed=8 * rows * block, transcendentals=0),
    )(where, weight, mod, xa, xb, total, grad)


def blank_kernel(out):
    pass


def ring_device(ring, x_first, x_layer, upstream, weight, bias):
    n = len(ring)
    half_way = n // 2
    block, samples = x_layer.shape
    half = block // 2
    parts = 2
    me = lax.axis_index("row")
    core = me % 2
    place = [0] * n
    for p, chip in enumerate(ring):
        place[chip] = p
    at = jnp.asarray(place, jnp.int32)[me // 2]
    order = jnp.asarray(ring, jnp.int32)

    def hop(by):
        return [(ring[p] * 2 + c, ring[(p + by) % n] * 2 + c) for p in range(n) for c in range(2)]

    swap = [(r, r ^ 1) for r in range(2 * n)]

    def send_up(v):
        return lax.ppermute(v, "row", hop(1))

    def send_down(v):
        return lax.ppermute(v, "row", hop(-1))

    def across(v):
        return lax.ppermute(v, "row", swap)

    def blocks_at(offset):
        chip = order[(at + offset + n) % n]
        return jnp.stack([chip * 2 + core, chip * 2 + 1 - core]).astype(jnp.int32)

    x_t = x_layer.T
    up_wide = upstream.astype(F32)
    mod_wide = lax.reduce_precision(up_wide * x_first.astype(F32), 8, 7)
    mod = mod_wide.astype(BF16)
    mod_t = mod.T
    bias_grad = jnp.sum(mod_wide, axis=1)

    held = {0: x_t}
    for s in range(1, half_way):
        held[-s] = send_up(held[1 - s])
        held[s] = send_down(held[s - 1])
    first = send_up(held[1 - half_way][:, :half])
    second = send_down(held[half_way - 1][:, half:])
    held[half_way] = jnp.concatenate([first, second], axis=1)

    offsets = [half_way]
    for s in range(half_way - 1, 0, -1):
        offsets += [s, -s]
    offsets.append(0)
    sums = {}
    for o in offsets:
        away, own = partials(blocks_at(o), mod_t, weight, block, parts)
        sums[o] = (own, across(away))

    def pair(o):
        own, other = sums[o]
        return own + other.astype(F32)

    far = pair(half_way)
    going_up = send_up(far[:, :half].astype(BF16))
    going_down = send_down(far[:, half:].astype(BF16))
    going_up = jnp.pad(going_up, ((0, 0), (0, block - half)))
    going_down = jnp.pad(going_down, ((0, 0), (half, 0)))
    for s in range(half_way - 1, 0, -1):
        going_up = send_up((pair(s) + going_up.astype(F32)).astype(BF16))
        going_down = send_down((pair(-s) + going_down.astype(F32)).astype(BF16))
    layer_grad = (pair(0) + going_up.astype(F32) + going_down.astype(F32)).astype(BF16).T

    rows = weight.shape[0]
    grad = pl.pallas_call(
        blank_kernel,
        out_specs=pl.BlockSpec(memory_space=pl.ANY),
        out_shape=jax.ShapeDtypeStruct(weight.shape, BF16),
    )()
    total = jnp.broadcast_to(bias[:, None], (rows, samples))
    for o in [0] + [sign * s for s in range(1, half_way) for sign in (-1, 1)] + [half_way]:
        total, grad = forward(blocks_at(o), weight, mod, held[o], across(held[o]), total, grad, parts)
    first_grad = (up_wide * total).astype(BF16)
    return (first_grad, layer_grad, grad, bias_grad)


def plain_device(x_first, x_layer, upstream, weight, bias):
    gathered = lax.all_gather(x_layer, "row", axis=0, tiled=True)
    affine = jnp.dot(weight, gathered, preferred_element_type=F32) + bias[:, None]
    up_wide = upstream.astype(F32)
    first_grad = (up_wide * affine).astype(BF16)
    modulated = (up_wide * x_first.astype(F32)).astype(BF16)
    weight_grad = lax.dot_general(modulated, gathered, (((1,), (1,)), ((), ())), preferred_element_type=F32).astype(BF16)
    bias_grad = jnp.sum(modulated.astype(F32), axis=1)
    share = lax.dot_general(weight, modulated, (((0,), (0,)), ((), ())), preferred_element_type=F32)
    layer_grad = lax.psum_scatter(share, "row", scatter_dimension=0, tiled=True).astype(BF16)
    return (first_grad, layer_grad, weight_grad, bias_grad)


def solution(mesh):
    chips = mesh.shape["row"] // 2
    on_device = functools.partial(ring_device, ring_of(chips)) if chips <= 16 else plain_device
    in_specs = (P("row", "group"), P("row", "group"), P("row", "group"), P("row", None), P("row"))
    out_specs = (
        P("row", "group"),
        P("row", "group"),
        P(("group", "row"), None),
        P(("group", "row")),
    )
    return jax.shard_map(
        on_device, mesh=mesh, in_specs=in_specs, out_specs=out_specs, check_vma=False
    )
```

time: 301 us -> 200 us (0.66)
  waiting for transfers between devices: 195 us -> 38.9 us
  Pallas kernels: 0 us -> 112 us
  matrix products: 89 us -> 0 us
  starting transfers between devices: 0.08 us -> 19.9 us
  other arithmetic: 2.88 us -> 10.9 us
  local copies, waits for them, and re-layouts: 0.01 us -> 6.55 us
    reduce_scatter x1 -> x0, waiting for transfers between devices: 139 us -> none  [on_device(): lax.psum_scatter(lax.dot_general(weight, modulated, (((0,), (0,)), ((), (...]
    pallas_call x0 -> x17, Pallas kernels: none -> 112 us  [the longest x8 67.6 us: forward(): pl.pallas_call(functools.partial(forward_kernel, parts), grid_spec=pltpu....]
    dot_general x3 -> x0, matrix products: 89 us -> none  [the longest x1 32.5 us: on_device(): lax.dot_general(modulated, gathered, (((1,), (1,)), ((), ())), preferred_...]
    all_gather x1 -> x0, waiting for transfers between devices: 55.2 us -> none  [on_device(): gathered = lax.all_gather(x_layer, 'row', axis=0, tiled=True)]
    ppermute x0 -> x32, waiting for transfers between devices: none -> 38.9 us  [the longest x8 37.7 us: send_down(): return lax.ppermute(v, 'row', hop(-1))]
    ppermute x0 -> x32, starting transfers between devices: none -> 19.9 us  [the longest x8 14.2 us: send_up(): return lax.ppermute(v, 'row', hop(1))]
  transfers between devices with their start and end apart: 2 -> 32, of which waited for: 2 -> 7; matrix products, arithmetic and copies ran while one was open for 30% -> 6% of each run, Pallas kernels for 0% -> 56%
where the time goes in v1:
time: 200 us; the launch traced here: 199 us
  Pallas kernels  112 us (56%)
  waiting for transfers between devices  38.9 us (19%)
  starting transfers between devices  19.9 us (10%)
  between operations  11.4 us (6%)
  other arithmetic  10.9 us (5%)
  local copies, waits for them, and re-layouts  6.55 us (3%)
    pallas_call x8, Pallas kernels, forward(): pl.pallas_call(functools.partial(forward_kernel, parts), grid_spec=pltpu....  67.6 us
    pallas_call x8, Pallas kernels, partials(): pl.pallas_call(functools.partial(partial_kernel, parts), grid_spec=pltpu....  44 us
    ppermute x8, waiting for transfers between devices, send_down(): return lax.ppermute(v, 'row', hop(-1))  37.7 us
    ppermute x8, starting transfers between devices, send_up(): return lax.ppermute(v, 'row', hop(1))  14.2 us
  transfers between devices with their start and end apart: 32, of which 7 were waited for; matrix products, arithmetic and copies ran while one was open for 6% of the time, Pallas kernels for 56%

profile of v1, /device:TPU:0, one launch (start us, length us, event | category | flops | bytes accessed | tf_op | source)
XLA Modules:
  0.0 199.2 jit_solution(16572067123085114406)
XLA Ops:
  1.1 2.6 %collective-permute-start = (bf16[192,1536]{1,0:T(8,128)(2,1)}, bf16[192,1536]{1,0:T(8,128)(2,1)}, u32[]{:S(2)}, u32[]{:S(2)}) collective-permute-start(bf16[192,1536]{1,0:T(8,128)(2,1)} %bitcast.45), channel_id=1, source_target_pairs={{2,6},{3,7},{6,10},{7,11},{10,14},{11,15},{14,12},{15,13},{12,8},{... | collective-permute-start | bytes 1769480 | tf_op jit(solution)/shard_map/ppermute | solution.py:132
  14.7 5.9 %shard_map.115 = (bf16[192,1536]{1,0:T(8,128)(2,1)}, f32[192,1536]{1,0:T(8,128)S(1)}) custom-call(s32[2]{0:T(128)S(1)} %pad_add_fusion.where, bf16[192,1024]{1,0:T(8,128)(2,1)S(1)} %bitcast.36, bf16[1024,24576]{1,0:T(8,128)(2,1)} %w.31), custom_call_target="tpu_custom_call" | custom-call | flops 1207959552 | bytes 6291456 | tf_op jit(solution)/shard_map/pallas_call | solution.py:40
  21.4 6.0 %shard_map.114 = (bf16[192,1536]{1,0:T(8,128)(2,1)}, f32[192,1536]{1,0:T(8,128)S(1)}) custom-call(s32[2]{0:T(128)S(1)} %pad_add_fusion.1.where, bf16[192,1024]{1,0:T(8,128)(2,1)S(1)} %bitcast.37, bf16[1024,24576]{1,0:T(8,128)(2,1)} %w.31), custom_call_target="tpu_custom_call" | custom-call | flops 1207959552 | bytes 6291456 | tf_op jit(solution)/shard_map/pallas_call | solution.py:40
  33.7 5.2 %shard_map.113 = (bf16[192,1536]{1,0:T(8,128)(2,1)S(1)}, f32[192,1536]{1,0:T(8,128)S(1)}) custom-call(s32[2]{0:T(128)S(1)} %pad_add_fusion.3.where, bf16[192,1024]{1,0:T(8,128)(2,1)S(1)} %bitcast.38, bf16[1024,24576]{1,0:T(8,128)(2,1)} %w.31), custom_call_target="tpu_custom_call" | custom-call | flops 1207959552 | bytes 6291456 | tf_op jit(solution)/shard_map/pallas_call | solution.py:40
  38.9 5.2 %shard_map.112 = (bf16[192,1536]{1,0:T(8,128)(2,1)S(1)}, f32[192,1536]{1,0:T(8,128)S(1)}) custom-call(s32[2]{0:T(128)S(1)} %pad_add_fusion.5.where, bf16[192,1024]{1,0:T(8,128)(2,1)S(1)} %bitcast.39, bf16[1024,24576]{1,0:T(8,128)(2,1)} %w.31), custom_call_target="tpu_custom_call" | custom-call | flops 1207959552 | bytes 6291456 | tf_op jit(solution)/shard_map/pallas_call | solution.py:40
  44.1 5.2 %shard_map.118 = (bf16[192,1536]{1,0:T(8,128)(2,1)S(1)}, f32[192,1536]{1,0:T(8,128)S(1)}) custom-call(s32[2]{0:T(128)S(1)} %pad_add_fusion.2.where, bf16[192,1024]{1,0:T(8,128)(2,1)S(1)} %bitcast.40, bf16[1024,24576]{1,0:T(8,128)(2,1)} %w.31), custom_call_target="tpu_custom_call" | custom-call | flops 1207959552 | bytes 6291456 | tf_op jit(solution)/shard_map/pallas_call | solution.py:40
  49.3 5.2 %shard_map.117 = (bf16[192,1536]{1,0:T(8,128)(2,1)S(1)}, f32[192,1536]{1,0:T(8,128)S(1)}) custom-call(s32[2]{0:T(128)S(1)} %pad_add_fusion.4.where, bf16[192,1024]{1,0:T(8,128)(2,1)S(1)} %bitcast.41, bf16[1024,24576]{1,0:T(8,128)(2,1)} %w.31), custom_call_target="tpu_custom_call" | custom-call | flops 1207959552 | bytes 6291456 | tf_op jit(solution)/shard_map/pallas_call | solution.py:40
  54.6 5.2 %shard_map.116 = (bf16[192,1536]{1,0:T(8,128)(2,1)S(1)}, f32[192,1536]{1,0:T(8,128)S(1)}) custom-call(s32[2]{0:T(128)S(1)} %pad_add_fusion.6.where, bf16[192,1024]{1,0:T(8,128)(2,1)S(1)} %bitcast.42, bf16[1024,24576]{1,0:T(8,128)(2,1)} %w.31), custom_call_target="tpu_custom_call" | custom-call | flops 1207959552 | bytes 6291456 | tf_op jit(solution)/shard_map/pallas_call | solution.py:40
  61.1 1.9 collective-permute-start.21
  63.0 6.0 %shard_map.111 = (bf16[192,1536]{1,0:T(8,128)(2,1)}, f32[192,1536]{1,0:T(8,128)S(1)}) custom-call(s32[2]{0:T(128)S(1)} %pad_add_fusion.7.where, bf16[192,1024]{1,0:T(8,128)(2,1)S(1)} %bitcast.43, bf16[1024,24576]{1,0:T(8,128)(2,1)} %w.31), custom_call_target="tpu_custom_call" | custom-call | flops 1207959552 | bytes 6291456 | tf_op jit(solution)/shard_map/pallas_call | solution.py:40
  70.0 8.4 %shard_map.103 = (f32[1024,192]{1,0:T(8,128)S(1)}, bf16[1024,24576]{1,0:T(8,128)(2,1)}) custom-call(s32[2]{0:T(128)S(1)} %pad_add_fusion.7.where, bf16[1024,24576]{1,0:T(8,128)(2,1)} %w.31, bf16[1024,192]{1,0:T(8,128)(2,1)S(1)} %copy.44.mod, bf16[192,1536]{1,0:T(8,128)(2,1)S(1)} %bitcast.47, ...), custom_call_target="tpu_custom_call", output_to_operand_aliasing={{0}: (5, {}), {1}: (6, {})} | custom-call | flops 2415919104 | bytes 12582912 | tf_op jit(solution)/shard_map/pallas_call | solution.py:83
  82.1 5.8 %collective-permute-done.28 = bf16[192,768]{1,0:T(8,128)(2,1)S(1)} collective-permute-done((bf16[192,768]{1,0:T(8,128)(2,1)S(1)}, bf16[192,768]{1,0:T(8,128)(2,1)S(1)}, u32[]{:S(2)}, u32[]{:S(2)}) %collective-permute-start.28) | collective-permute-done | bytes 294944 | tf_op jit(solution)/shard_map/ppermute | solution.py:135
  89.7 8.5 %shard_map.104 = (f32[1024,192]{1,0:T(8,128)S(1)}, bf16[1024,24576]{1,0:T(8,128)(2,1)}) custom-call(s32[2]{0:T(128)S(1)} %pad_add_fusion.6.where, bf16[1024,24576]{1,0:T(8,128)(2,1)} %w.31, bf16[1024,192]{1,0:T(8,128)(2,1)S(1)} %copy.44.mod, bf16[192,1536]{1,0:T(8,128)(2,1)} %collective-permute-done.xa, ...), custom_call_target="tpu_custom_call", output_to_operand_aliasing={{0}: (5, {}), {1}: (6, {})} | custom-call | flops 2415919104 | bytes 12582912 | tf_op jit(solution)/shard_map/pallas_call | solution.py:83
  98.9 8.5 %shard_map.105 = (f32[1024,192]{1,0:T(8,128)S(1)}, bf16[1024,24576]{1,0:T(8,128)(2,1)}) custom-call(s32[2]{0:T(128)S(1)} %pad_add_fusion.5.where, bf16[1024,24576]{1,0:T(8,128)(2,1)} %w.31, bf16[1024,192]{1,0:T(8,128)(2,1)S(1)} %copy.44.mod, bf16[192,1536]{1,0:T(8,128)(2,1)} %collective-permute-done.4.xa, ...), custom_call_target="tpu_custom_call", output_to_operand_aliasing={{0}: (5, {}), {1}: (6, {})} | custom-call | flops 2415919104 | bytes 12582912 | tf_op jit(solution)/shard_map/pallas_call | solution.py:83
  110.7 3.8 %collective-permute-done.5.xa = bf16[192,1536]{1,0:T(8,128)(2,1)S(1)} collective-permute-done((bf16[192,1536]{1,0:T(8,128)(2,1)}, bf16[192,1536]{1,0:T(8,128)(2,1)S(1)}, u32[]{:S(2)}, u32[]{:S(2)}) %collective-permute-start.5) | collective-permute-done | bytes 589856 | tf_op jit(solution)/shard_map/ppermute | solution.py:135
  114.6 12.2 %collective-permute-done.29 = bf16[192,1536]{1,0:T(8,128)(2,1)S(1)} collective-permute-done((bf16[192,1536]{1,0:T(8,128)(2,1)S(1)}, bf16[192,1536]{1,0:T(8,128)(2,1)S(1)}, u32[]{:S(2)}, u32[]{:S(2)}) %collective-permute-start.29) | collective-permute-done | bytes 589856 | tf_op jit(solution)/shard_map/ppermute | solution.py:135
  130.8 8.4 %shard_map.106 = (f32[1024,192]{1,0:T(8,128)S(1)}, bf16[1024,24576]{1,0:T(8,128)(2,1)}) custom-call(s32[2]{0:T(128)S(1)} %pad_add_fusion.4.where, bf16[1024,24576]{1,0:T(8,128)(2,1)} %w.31, bf16[1024,192]{1,0:T(8,128)(2,1)S(1)} %copy.44.mod, bf16[192,1536]{1,0:T(8,128)(2,1)S(1)} %collective-permute-done.1.xa, ...), custom_call_target="tpu_custom_call", output_to_operand_aliasing={{0}: (5, {}), {1}: (6, {})} | custom-call | flops 2415919104 | bytes 12582912 | tf_op jit(solution)/shard_map/pallas_call | solution.py:83
  139.2 2.5 %collective-permute-done.6.xa = bf16[192,1536]{1,0:T(8,128)(2,1)S(1)} collective-permute-done((bf16[192,1536]{1,0:T(8,128)(2,1)S(1)}, bf16[192,1536]{1,0:T(8,128)(2,1)S(1)}, u32[]{:S(2)}, u32[]{:S(2)}) %collective-permute-start.6) | collective-permute-done | bytes 589856 | tf_op jit(solution)/shard_map/ppermute | solution.py:135
  142.3 8.4 %shard_map.107 = (f32[1024,192]{1,0:T(8,128)S(1)}, bf16[1024,24576]{1,0:T(8,128)(2,1)}) custom-call(s32[2]{0:T(128)S(1)} %copy-done.10, bf16[1024,24576]{1,0:T(8,128)(2,1)} %w.31, bf16[1024,192]{1,0:T(8,128)(2,1)S(1)} %copy.44.mod, bf16[192,1536]{1,0:T(8,128)(2,1)S(1)} %collective-permute-done.5.xa, ...), custom_call_target="tpu_custom_call", output_to_operand_aliasing={{0}: (5, {}), {1}: (6, {})} | custom-call | flops 2415919104 | bytes 12582912 | tf_op jit(solution)/shard_map/pallas_call | solution.py:83
  153.4 13.1 %collective-permute-done.30 = bf16[192,1536]{1,0:T(8,128)(2,1)S(1)} collective-permute-done((bf16[192,1536]{1,0:T(8,128)(2,1)S(1)}, bf16[192,1536]{1,0:T(8,128)(2,1)S(1)}, u32[]{:S(2)}, u32[]{:S(2)}) %collective-permute-start.30) | collective-permute-done | bytes 589856 | tf_op jit(solution)/shard_map/ppermute | solution.py:135
  169.6 8.4 %shard_map.108 = (f32[1024,192]{1,0:T(8,128)S(1)}, bf16[1024,24576]{1,0:T(8,128)(2,1)}) custom-call(s32[2]{0:T(128)S(1)} %copy-done.8, bf16[1024,24576]{1,0:T(8,128)(2,1)} %w.31, bf16[1024,192]{1,0:T(8,128)(2,1)S(1)} %copy.44.mod, bf16[192,1536]{1,0:T(8,128)(2,1)S(1)} %collective-permute-done.2.xa, ...), custom_call_target="tpu_custom_call", output_to_operand_aliasing={{0}: (5, {}), {1}: (6, {})} | custom-call | flops 2415919104 | bytes 12582912 | tf_op jit(solution)/shard_map/pallas_call | solution.py:83
  178.0 8.4 %shard_map.109 = (f32[1024,192]{1,0:T(8,128)S(1)}, bf16[1024,24576]{1,0:T(8,128)(2,1)}) custom-call(s32[2]{0:T(128)S(1)} %copy-done.6, bf16[1024,24576]{1,0:T(8,128)(2,1)} %w.31, bf16[1024,192]{1,0:T(8,128)(2,1)S(1)} %copy.44.mod, bf16[192,1536]{1,0:T(8,128)(2,1)S(1)} %collective-permute-done.6.xa, ...), custom_call_target="tpu_custom_call", output_to_operand_aliasing={{0}: (5, {}), {1}: (6, {})} | custom-call | flops 2415919104 | bytes 12582912 | tf_op jit(solution)/shard_map/pallas_call | solution.py:83
  186.5 8.4 %shard_map.110 = (f32[1024,192]{1,0:T(8,128)S(1)}, bf16[1024,24576]{1,0:T(8,128)(2,1)}) custom-call(s32[2]{0:T(128)S(1)} %copy-done.4, bf16[1024,24576]{1,0:T(8,128)(2,1)} %w.31, bf16[1024,192]{1,0:T(8,128)(2,1)S(1)} %copy.44.mod, bf16[192,1536]{1,0:T(8,128)(2,1)S(1)} %constant_dynamic-update-slice_fusion.xa, ...), custom_call_target="tpu_custom_call", output_to_operand_aliasing={{0}: (5, {}), {1}: (6, {})} | custom-call | flops 2415919104 | bytes 12582912 | tf_op jit(solution)/shard_map/pallas_call | solution.py:83
  196.7 2.5 %fusion.4 = bf16[1536,192]{0,1:T(8,128)(2,1)} fusion(bf16[192,1536]{1,0:T(8,128)(2,1)} %collective-permute-done.31, bf16[192,1536]{1,0:T(8,128)(2,1)} %collective-permute-done.24, f32[192,1536]{1,0:T(8,128)S(1)} %get-tuple-element.51, bf16[192,1536]{1,0:T(8,128)(2,1)} %collective-permute-done.16), kind=kLoop, calls=%fused_computation.14 | loop fusion | flops 2064384 | bytes 3538944 | tf_op jit(solution)/shard_map/transpose | solution.py:180
  (111 shorter events, 31.8 us)
Async XLA Ops:
  0.6 68.3 %collective-permute-start.15 = (bf16[192,1536]{1,0:T(8,128)(2,1)}, bf16[192,1536]{1,0:T(8,128)(2,1)S(1)}, u32[]{:S(2)}, u32[]{:S(2)}) collective-permute-start(bf16[192,1536]{1,0:T(8,128)(2,1)} %bitcast.44), channel_id=1, source_target_pairs={{0,1},{1,0},{2,3},{3,2},{4,5},{5,4},{6,7},{7,6},{8,9},{9,8},{10,11... | collective-permute-start | bytes 1769480 | tf_op jit(solution)/shard_map/ppermute | solution.py:138
  1.1 77.3 %collective-permute-start = (bf16[192,1536]{1,0:T(8,128)(2,1)}, bf16[192,1536]{1,0:T(8,128)(2,1)}, u32[]{:S(2)}, u32[]{:S(2)}) collective-permute-start(bf16[192,1536]{1,0:T(8,128)(2,1)} %bitcast.45), channel_id=1, source_target_pairs={{2,6},{3,7},{6,10},{7,11},{10,14},{11,15},{14,12},{15,13},{12,8},{... | collective-permute-start | bytes 1769480 | tf_op jit(solution)/shard_map/ppermute | solution.py:132
  3.7 76.6 %collective-permute-start.4 = (bf16[192,1536]{1,0:T(8,128)(2,1)}, bf16[192,1536]{1,0:T(8,128)(2,1)}, u32[]{:S(2)}, u32[]{:S(2)}) collective-permute-start(bf16[192,1536]{1,0:T(8,128)(2,1)} %bitcast.46), channel_id=1, source_target_pairs={{2,0},{3,1},{6,2},{7,3},{10,6},{11,7},{14,10},{15,11},{12,14},{13,... | collective-permute-start | bytes 1769480 | tf_op jit(solution)/shard_map/ppermute | solution.py:135
  20.6 39.2 %collective-permute-start.20 = (bf16[192,1536]{1,0:T(8,128)(2,1)}, bf16[192,1536]{1,0:T(8,128)(2,1)}, u32[]{:S(2)}, u32[]{:S(2)}) collective-permute-start(bf16[192,1536]{1,0:T(8,128)(2,1)} %get-tuple-element.60), channel_id=1, source_target_pairs={{0,1},{1,0},{2,3},{3,2},{4,5},{5,4},{6,7},{7,6},{8,9},{9,8},{10,11... | collective-permute-start | bytes 1769480 | tf_op jit(solution)/shard_map/ppermute | solution.py:138
  28.5 50.0 %collective-permute-start.19 = (bf16[192,1536]{1,0:T(8,128)(2,1)}, bf16[192,1536]{1,0:T(8,128)(2,1)}, u32[]{:S(2)}, u32[]{:S(2)}) collective-permute-start(bf16[192,1536]{1,0:T(8,128)(2,1)} %get-tuple-element.58), channel_id=1, source_target_pairs={{0,1},{1,0},{2,3},{3,2},{4,5},{5,4},{6,7},{7,6},{8,9},{9,8},{10,11... | collective-permute-start | bytes 1769480 | tf_op jit(solution)/shard_map/ppermute | solution.py:138
  61.1 17.6 %collective-permute-start.21 = (bf16[192,768]{1,0:T(8,128)(2,1)S(1)}, bf16[192,768]{1,0:T(8,128)(2,1)S(1)}, u32[]{:S(2)}, u32[]{:S(2)}) collective-permute-start(bf16[192,768]{1,0:T(8,128)(2,1)S(1)} %get-tuple-element.70), channel_id=1, source_target_pairs={{2,6},{3,7},{6,10},{7,11},{10,14},{11,15},{14,12},{15,13},{12,8},{... | collective-permute-start | bytes 884744 | tf_op jit(solution)/shard_map/ppermute | solution.py:132
  78.4 19.8 %collective-permute-start.18 = (bf16[192,1536]{1,0:T(8,128)(2,1)S(1)}, bf16[192,1536]{1,0:T(8,128)(2,1)S(1)}, u32[]{:S(2)}, u32[]{:S(2)}) collective-permute-start(bf16[192,1536]{1,0:T(8,128)(2,1)S(1)} %get-tuple-element.56), channel_id=1, source_target_pairs={{0,1},{1,0},{2,3},{3,2},{4,5},{5,4},{6,7},{7,6},{8,9},{9,8},{10,11... | collective-permute-start | bytes 1769480 | tf_op jit(solution)/shard_map/ppermute | solution.py:138
  80.3 27.2 %collective-permute-start.1 = (bf16[192,1536]{1,0:T(8,128)(2,1)}, bf16[192,1536]{1,0:T(8,128)(2,1)S(1)}, u32[]{:S(2)}, u32[]{:S(2)}) collective-permute-start(bf16[192,1536]{1,0:T(8,128)(2,1)} %collective-permute-done.xa), channel_id=1, source_target_pairs={{2,6},{3,7},{6,10},{7,11},{10,14},{11,15},{14,12},{15,13},{12,8},{... | collective-permute-start | bytes 1769480 | tf_op jit(solution)/shard_map/ppermute | solution.py:132
  82.0 16.7 %collective-permute-start.13 = (bf16[192,1536]{1,0:T(8,128)(2,1)}, bf16[192,1536]{1,0:T(8,128)(2,1)S(1)}, u32[]{:S(2)}, u32[]{:S(2)}) collective-permute-start(bf16[192,1536]{1,0:T(8,128)(2,1)} %collective-permute-done.4.xa), channel_id=1, source_target_pairs={{0,1},{1,0},{2,3},{3,2},{4,5},{5,4},{6,7},{7,6},{8,9},{9,8},{10,11... | collective-permute-start | bytes 1769480 | tf_op jit(solution)/shard_map/ppermute | solution.py:138
  87.9 20.9 %collective-permute-start.22 = (bf16[192,1536]{1,0:T(8,128)(2,1)S(1)}, bf16[192,1536]{1,0:T(8,128)(2,1)S(1)}, u32[]{:S(2)}, u32[]{:S(2)}) collective-permute-start(bf16[192,1536]{1,0:T(8,128)(2,1)S(1)} %add_convert_fusion.6), channel_id=1, source_target_pairs={{2,6},{3,7},{6,10},{7,11},{10,14},{11,15},{14,12},{15,13},{12,8},{... | collective-permute-start | bytes 1769480 | tf_op jit(solution)/shard_map/ppermute | solution.py:132
  89.6 21.1 %collective-permute-start.26 = (bf16[192,1536]{1,0:T(8,128)(2,1)S(1)}, bf16[192,1536]{1,0:T(8,128)(2,1)S(1)}, u32[]{:S(2)}, u32[]{:S(2)}) collective-permute-start(bf16[192,1536]{1,0:T(8,128)(2,1)S(1)} %get-tuple-element.64), channel_id=1, source_target_pairs={{0,1},{1,0},{2,3},{3,2},{4,5},{5,4},{6,7},{7,6},{8,9},{9,8},{10,11... | collective-permute-start | bytes 1769480 | tf_op jit(solution)/shard_map/ppermute | solution.py:138
  98.7 28.1 %collective-permute-start.29 = (bf16[192,1536]{1,0:T(8,128)(2,1)S(1)}, bf16[192,1536]{1,0:T(8,128)(2,1)S(1)}, u32[]{:S(2)}, u32[]{:S(2)}) collective-permute-start(bf16[192,1536]{1,0:T(8,128)(2,1)S(1)} %add_convert_fusion.3), channel_id=1, source_target_pairs={{2,0},{3,1},{6,2},{7,3},{10,6},{11,7},{14,10},{15,11},{12,14},{13,... | collective-permute-start | bytes 1769480 | tf_op jit(solution)/shard_map/ppermute | solution.py:135
  107.5 21.6 %collective-permute-start.12 = (bf16[192,1536]{1,0:T(8,128)(2,1)S(1)}, bf16[192,1536]{1,0:T(8,128)(2,1)S(1)}, u32[]{:S(2)}, u32[]{:S(2)}) collective-permute-start(bf16[192,1536]{1,0:T(8,128)(2,1)S(1)} %collective-permute-done.1.xa), channel_id=1, source_target_pairs={{0,1},{1,0},{2,3},{3,2},{4,5},{5,4},{6,7},{7,6},{8,9},{9,8},{10,11... | collective-permute-start | bytes 1769480 | tf_op jit(solution)/shard_map/ppermute | solution.py:138
  108.8 18.7 %collective-permute-start.2 = (bf16[192,1536]{1,0:T(8,128)(2,1)S(1)}, bf16[192,1536]{1,0:T(8,128)(2,1)S(1)}, u32[]{:S(2)}, u32[]{:S(2)}) collective-permute-start(bf16[192,1536]{1,0:T(8,128)(2,1)S(1)} %collective-permute-done.1.xa), channel_id=1, source_target_pairs={{2,6},{3,7},{6,10},{7,11},{10,14},{11,15},{14,12},{15,13},{12,8},{... | collective-permute-start | bytes 1769480 | tf_op jit(solution)/shard_map/ppermute | solution.py:132
  110.7 41.1 %collective-permute-start.17 = (bf16[192,1536]{1,0:T(8,128)(2,1)S(1)}, bf16[192,1536]{1,0:T(8,128)(2,1)S(1)}, u32[]{:S(2)}, u32[]{:S(2)}) collective-permute-start(bf16[192,1536]{1,0:T(8,128)(2,1)S(1)} %get-tuple-element.54), channel_id=1, source_target_pairs={{0,1},{1,0},{2,3},{3,2},{4,5},{5,4},{6,7},{7,6},{8,9},{9,8},{10,11... | collective-permute-start | bytes 1769480 | tf_op jit(solution)/shard_map/ppermute | solution.py:138
  114.6 27.2 %collective-permute-start.11 = (bf16[192,1536]{1,0:T(8,128)(2,1)S(1)}, bf16[192,1536]{1,0:T(8,128)(2,1)S(1)}, u32[]{:S(2)}, u32[]{:S(2)}) collective-permute-start(bf16[192,1536]{1,0:T(8,128)(2,1)S(1)} %collective-permute-done.5.xa), channel_id=1, source_target_pairs={{0,1},{1,0},{2,3},{3,2},{4,5},{5,4},{6,7},{7,6},{8,9},{9,8},{10,11... | collective-permute-start | bytes 1769480 | tf_op jit(solution)/shard_map/ppermute | solution.py:138
  127.5 24.4 %collective-permute-start.23 = (bf16[192,1536]{1,0:T(8,128)(2,1)S(1)}, bf16[192,1536]{1,0:T(8,128)(2,1)S(1)}, u32[]{:S(2)}, u32[]{:S(2)}) collective-permute-start(bf16[192,1536]{1,0:T(8,128)(2,1)S(1)} %add_convert_fusion.5), channel_id=1, source_target_pairs={{2,6},{3,7},{6,10},{7,11},{10,14},{11,15},{14,12},{15,13},{12,8},{... | collective-permute-start | bytes 1769480 | tf_op jit(solution)/shard_map/ppermute | solution.py:132
  129.1 21.6 %collective-permute-start.3 = (bf16[192,768]{1,0:T(8,128)(2,1)S(1)}, bf16[192,768]{1,0:T(8,128)(2,1)S(1)}, u32[]{:S(2)}, u32[]{:S(2)}) collective-permute-start(bf16[192,768]{1,0:T(8,128)(2,1)S(1)} %slice.18), channel_id=1, source_target_pairs={{2,6},{3,7},{6,10},{7,11},{10,14},{11,15},{14,12},{15,13},{12,8},{... | collective-permute-start | bytes 884744 | tf_op jit(solution)/shard_map/ppermute | solution.py:132
  150.7 46.0 %collective-permute-start.16 = (bf16[192,1536]{1,0:T(8,128)(2,1)}, bf16[192,1536]{1,0:T(8,128)(2,1)}, u32[]{:S(2)}, u32[]{:S(2)}) collective-permute-start(bf16[192,1536]{1,0:T(8,128)(2,1)} %get-tuple-element.52), channel_id=1, source_target_pairs={{0,1},{1,0},{2,3},{3,2},{4,5},{5,4},{6,7},{7,6},{8,9},{9,8},{10,11... | collective-permute-start | bytes 1769480 | tf_op jit(solution)/shard_map/ppermute | solution.py:138
  151.7 17.4 %collective-permute-start.10 = (bf16[192,1536]{1,0:T(8,128)(2,1)S(1)}, bf16[192,1536]{1,0:T(8,128)(2,1)S(1)}, u32[]{:S(2)}, u32[]{:S(2)}) collective-permute-start(bf16[192,1536]{1,0:T(8,128)(2,1)S(1)} %collective-permute-done.2.xa), channel_id=1, source_target_pairs={{0,1},{1,0},{2,3},{3,2},{4,5},{5,4},{6,7},{7,6},{8,9},{9,8},{10,11... | collective-permute-start | bytes 1769480 | tf_op jit(solution)/shard_map/ppermute | solution.py:138
  151.8 26.2 %collective-permute-start.9 = (bf16[192,1536]{1,0:T(8,128)(2,1)S(1)}, bf16[192,1536]{1,0:T(8,128)(2,1)S(1)}, u32[]{:S(2)}, u32[]{:S(2)}) collective-permute-start(bf16[192,1536]{1,0:T(8,128)(2,1)S(1)} %collective-permute-done.6.xa), channel_id=1, source_target_pairs={{0,1},{1,0},{2,3},{3,2},{4,5},{5,4},{6,7},{7,6},{8,9},{9,8},{10,11... | collective-permute-start | bytes 1769480 | tf_op jit(solution)/shard_map/ppermute | solution.py:138
  153.4 33.1 %collective-permute-start.8 = (bf16[192,1536]{1,0:T(8,128)(2,1)S(1)}, bf16[192,1536]{1,0:T(8,128)(2,1)S(1)}, u32[]{:S(2)}, u32[]{:S(2)}) collective-permute-start(bf16[192,1536]{1,0:T(8,128)(2,1)S(1)} %constant_dynamic-update-slice_fusion.xa), channel_id=1, source_target_pairs={{0,1},{1,0},{2,3},{3,2},{4,5},{5,4},{6,7},{7,6},{8,9},{9,8},{10,11... | collective-permute-start | bytes 1769480 | tf_op jit(solution)/shard_map/ppermute | solution.py:138
  166.5 30.2 %collective-permute-start.24 = (bf16[192,1536]{1,0:T(8,128)(2,1)}, bf16[192,1536]{1,0:T(8,128)(2,1)}, u32[]{:S(2)}, u32[]{:S(2)}) collective-permute-start(bf16[192,1536]{1,0:T(8,128)(2,1)} %add_convert_fusion.4), channel_id=1, source_target_pairs={{2,6},{3,7},{6,10},{7,11},{10,14},{11,15},{14,12},{15,13},{12,8},{... | collective-permute-start | bytes 1769480 | tf_op jit(solution)/shard_map/ppermute | solution.py:132
  169.1 27.6 %collective-permute-start.31 = (bf16[192,1536]{1,0:T(8,128)(2,1)}, bf16[192,1536]{1,0:T(8,128)(2,1)}, u32[]{:S(2)}, u32[]{:S(2)}) collective-permute-start(bf16[192,1536]{1,0:T(8,128)(2,1)} %add_convert_fusion.1), channel_id=1, source_target_pairs={{2,0},{3,1},{6,2},{7,3},{10,6},{11,7},{14,10},{15,11},{12,14},{13,... | collective-permute-start | bytes 1769480 | tf_op jit(solution)/shard_map/ppermute | solution.py:135
  (21 other events, 174.4 us)

commit v2 on v0

v2 whole, which is shorter than its diff:
```python
import functools

import jax
import jax.numpy as jnp
from jax import lax
from jax.experimental import pallas as pl
from jax.experimental.pallas import tpu as pltpu
from jax.sharding import PartitionSpec as P

F32 = jnp.float32
BF16 = jnp.bfloat16


def ring_of(n):
    width = {8: 2, 64: 4}.get(n, 2)
    depth = n // width
    walk = []
    for z in range(depth):
        xs = list(range(1, width))
        walk += [z * width + x for x in (xs if z % 2 == 0 else xs[::-1])]
    return walk + [z * width for z in reversed(range(depth))]


ANYWHERE = pl.BlockSpec(memory_space=pl.ANY)


TOKEN = jax.ShapeDtypeStruct((8, 128), F32)


def partial_kernel(k, where, mod_t, w, *refs):
    away, own = refs[-3:-1]
    t = pl.program_id(0)
    out = jnp.dot(mod_t[...], w[...], preferred_element_type=F32)

    @pl.when(t < k)
    def _():
        away[...] = out.astype(away.dtype)

    @pl.when(t >= k)
    def _():
        own[...] = out


def partials(where, base, k, mod_t, weight, block, after):
    samples, rows = mod_t.shape
    return pl.pallas_call(
        functools.partial(partial_kernel, k),
        grid_spec=pltpu.PrefetchScalarGridSpec(
            num_scalar_prefetch=1,
            grid=(2 * k,),
            in_specs=[
                pl.BlockSpec((samples, rows), lambda t, s: (0, 0)),
                pl.BlockSpec((rows, block), lambda t, s: (0, s[base + t])),
            ]
            + [ANYWHERE] * len(after),
            out_specs=[
                pl.BlockSpec((None, samples, block), lambda t, s: (jnp.minimum(t, k - 1), 0, 0)),
                pl.BlockSpec((None, samples, block), lambda t, s: (jnp.maximum(t - k, 0), 0, 0)),
                ANYWHERE,
            ],
        ),
        out_shape=[jax.ShapeDtypeStruct((k, samples, block), BF16), jax.ShapeDtypeStruct((k, samples, block), F32), TOKEN],
        compiler_params=pltpu.CompilerParams(vmem_limit_bytes=24 << 20),
        cost_estimate=pl.CostEstimate(
            flops=4 * k * samples * rows * block, bytes_accessed=4 * k * rows * block, transcendentals=0
        ),
    )(where, mod_t, weight, *after)


def forward_kernel(k, chained, where, w, mod, *refs):
    xs, (total, grad) = refs[:k], refs[-3:-1]
    t = pl.program_id(0)

    @pl.when(t == 0)
    def _():
        total[...] = refs[k][...] if chained else jnp.zeros_like(total)

    def step(x):
        total[...] += lax.dot_general(x[...], w[...], (((1,), (1,)), ((), ())), preferred_element_type=F32)
        grad[...] = jnp.dot(mod[...], x[...], preferred_element_type=F32).astype(grad.dtype)

    for i in range(k):
        pl.when(t == i)(functools.partial(step, xs[i]))


def forward(where, base, weight, mod, xs, carry, after):
    rows, samples = mod.shape
    block = xs[0].shape[1]
    k = len(xs)
    whole = pl.BlockSpec((samples, rows), lambda t, s: (0, 0))
    column = pl.BlockSpec((rows, block), lambda t, s: (0, s[base + t]))
    return pl.pallas_call(
        functools.partial(forward_kernel, k, bool(carry)),
        grid_spec=pltpu.PrefetchScalarGridSpec(
            num_scalar_prefetch=1,
            grid=(k,),
            in_specs=[column, pl.BlockSpec((rows, samples), lambda t, s: (0, 0))]
            + [pl.BlockSpec((samples, block), lambda t, s: (0, 0))] * k
            + ([whole, ANYWHERE] if carry else [])
            + [ANYWHERE] * len(after),
            out_specs=[whole, column, ANYWHERE],
        ),
        out_shape=[jax.ShapeDtypeStruct((samples, rows), F32), jax.ShapeDtypeStruct(weight.shape, BF16), TOKEN],
        input_output_aliases={3 + k: 0, 4 + k: 1} if carry else {},
        compiler_params=pltpu.CompilerParams(vmem_limit_bytes=40 << 20),
        cost_estimate=pl.CostEstimate(
            flops=4 * k * samples * rows * block, bytes_accessed=4 * k * rows * block, transcendentals=0
        ),
    )(where, weight, mod, *xs, *carry, *after)


def ring_device(ring, x_first, x_layer, upstream, weight, bias):
    n = len(ring)
    far = n // 2
    block = x_layer.shape[0]
    half = block // 2

    def hop(by):
        return [(ring[p] * 2 + c, ring[(p + by) % n] * 2 + c) for p in range(n) for c in range(2)]

    swap = [(r, r ^ 1) for r in range(2 * n)]

    def send_up(v):
        return lax.ppermute(v, "row", hop(1))

    def send_down(v):
        return lax.ppermute(v, "row", hop(-1))

    def across(v):
        return lax.ppermute(v, "row", swap)

    near = [[0, -1, 1]] + [[-s, s] for s in range(2, far)] + [[far]]
    outer = [[far, far - 1, 1 - far]] + [[2, -2, 1], [-1, 0]]
    table, bases, fill = [], {}, 0
    for name, group in [("p%d" % i, g) for i, g in enumerate(outer)] + [("f%d" % i, g) for i, g in enumerate(near)]:
        bases[name] = fill
        fill += 2 * len(group)
    for r in range(2 * n):
        p, core = ring.index(r // 2), r % 2
        line = []
        for group in outer:
            chips = [ring[(p + o) % n] for o in group]
            line += [chip * 2 + 1 - core for chip in chips] + [chip * 2 + core for chip in chips]
        for group in near:
            for o in group:
                chip = ring[(p + o) % n]
                line += [chip * 2 + core, chip * 2 + 1 - core]
        table.append(line)
    where = jnp.asarray(table, jnp.int32)[lax.axis_index("row")]

    x_t = x_layer.T
    up_t = upstream.T.astype(F32)
    mod_wide = lax.reduce_precision(up_t * x_first.T.astype(F32), 8, 7)
    mod_t = mod_wide.astype(BF16)
    mod = mod_t.T
    bias_grad = jnp.sum(mod_wide, axis=0)

    held, other = {0: x_t}, {0: across(x_t)}
    sums = {}

    def gather_step(s):
        up, down = held[1 - s], held[s - 1]
        if s == far:
            up, down = up[:, :half], down[:, half:]
        return [send_up(up), send_down(down)]

    def gathered(s, arrived):
        if s == far:
            held[far] = jnp.concatenate(arrived, axis=1)
            other[far] = across(held[far])
        else:
            held[-s], held[s] = arrived
            other[-s], other[s] = across(held[-s]), across(held[s])

    def share(i, away, own):
        back = across(away)
        for j, o in enumerate(outer[i]):
            sums[o] = (own, back, j)
        return back

    def partial_group(i, after):
        return partials(where, bases["p%d" % i], len(outer[i]), mod_t, weight, block, after)

    def pair(o):
        own, back, j = sums[o]
        return own[j] + back[j].astype(F32)

    def forward_group(i, carry, after):
        xs = [v for o in near[i] for v in (held[o], other[o])]
        return forward(where, bases["f%d" % i], weight, mod, xs, carry, after)

    def reduce_step(s, ups, downs):
        if s == far:
            both = pair(far)
            ups = send_up(both[:, :half].astype(BF16))
            downs = send_down(both[:, half:].astype(BF16))
        elif s == far - 1:
            ups = jnp.pad(ups, ((0, 0), (0, block - half)))
            downs = jnp.pad(downs, ((0, 0), (half, 0)))
            ups = send_up((pair(s) + ups.astype(F32)).astype(BF16))
            downs = send_down((pair(-s) + downs.astype(F32)).astype(BF16))
        else:
            ups = send_up((pair(s) + ups.astype(F32)).astype(BF16))
            downs = send_down((pair(-s) + downs.astype(F32)).astype(BF16))
        return ups, downs

    first = gather_step(1)
    away, own, _ = partial_group(0, [])
    away, *first = lax.optimization_barrier((away, *first))
    gathered(1, first)
    back = share(0, away, own)
    second = gather_step(2)
    away, own, token = partial_group(1, first)
    *second, token = lax.optimization_barrier((*second, token))
    share(1, away, own)
    gathered(2, second)
    third = gather_step(3)
    ups, downs = reduce_step(4, None, None)
    away, own, later = partial_group(2, [*second, back, token])
    share(2, away, own)
    *third, later = lax.optimization_barrier((*third, later))
    gathered(3, third)
    fourth = gather_step(4)
    ups, downs = reduce_step(3, ups, downs)
    *carry, token = forward_group(0, [], [*third, later])
    gathered(4, fourth)
    *carry, _ = forward_group(1, carry, [*fourth, ups, downs])
    ups, downs = reduce_step(2, ups, downs)
    *carry, _ = forward_group(2, carry, [ups, downs])
    ups, downs = reduce_step(1, ups, downs)
    *carry, _ = forward_group(3, carry, [])
    layer_grad = (pair(0) + ups.astype(F32) + downs.astype(F32)).astype(BF16).T
    total, grad = carry
    first_grad = (up_t * (total + bias[None, :])).astype(BF16).T
    return (first_grad, layer_grad, grad, bias_grad)


def plain_device(x_first, x_layer, upstream, weight, bias):
    gathered = lax.all_gather(x_layer, "row", axis=0, tiled=True)
    affine = jnp.dot(weight, gathered, preferred_element_type=F32) + bias[:, None]
    up_wide = upstream.astype(F32)
    first_grad = (up_wide * affine).astype(BF16)
    modulated = (up_wide * x_first.astype(F32)).astype(BF16)
    weight_grad = lax.dot_general(modulated, gathered, (((1,), (1,)), ((), ())), preferred_element_type=F32).astype(BF16)
    bias_grad = jnp.sum(modulated.astype(F32), axis=1)
    share = lax.dot_general(weight, modulated, (((0,), (0,)), ((), ())), preferred_element_type=F32)
    layer_grad = lax.psum_scatter(share, "row", scatter_dimension=0, tiled=True).astype(BF16)
    return (first_grad, layer_grad, weight_grad, bias_grad)


def solution(mesh):
    chips = mesh.shape["row"] // 2
    on_device = functools.partial(ring_device, ring_of(chips)) if chips == 8 else plain_device
    in_specs = (P("row", "group"), P("row", "group"), P("row", "group"), P("row", None), P("row"))
    out_specs = (
        P("row", "group"),
        P("row", "group"),
        P(("group", "row"), None),
        P(("group", "row")),
    )
    return jax.shard_map(
        on_device, mesh=mesh, in_specs=in_specs, out_specs=out_specs, check_vma=False
    )
```

time: 301 us -> 144 us (0.48)
  waiting for transfers between devices: 195 us -> 28.5 us
  matrix products: 89 us -> 0 us
  Pallas kernels: 0 us -> 82 us
  starting transfers between devices: 0.08 us -> 19.3 us
  between operations: 14.1 us -> 0.83 us
  other arithmetic: 2.88 us -> 8.1 us
  local copies, waits for them, and re-layouts: 0.01 us -> 4.71 us
    reduce_scatter x1 -> x0, waiting for transfers between devices: 139 us -> none  [on_device(): lax.psum_scatter(lax.dot_general(weight, modulated, (((0,), (0,)), ((), (...]
    dot_general x3 -> x0, matrix products: 89 us -> none  [the longest x1 32.5 us: on_device(): lax.dot_general(modulated, gathered, (((1,), (1,)), ((), ())), preferred_...]
    pallas_call x0 -> x7, Pallas kernels: none -> 82 us  [the longest x4 54.3 us: forward(): pl.pallas_call(functools.partial(forward_kernel, k, bool(carry)), grid_sp...]
    all_gather x1 -> x0, waiting for transfers between devices: 55.2 us -> none  [on_device(): gathered = lax.all_gather(x_layer, 'row', axis=0, tiled=True)]
    ppermute x0 -> x27, waiting for transfers between devices: none -> 28.5 us  [the longest x8 22.5 us: send_up(): return lax.ppermute(v, 'row', hop(1))]
    ppermute x0 -> x27, starting transfers between devices: none -> 19.3 us  [the longest x8 14.1 us: send_up(): return lax.ppermute(v, 'row', hop(1))]
    transpose x0 -> x2, other arithmetic: none -> 4.06 us  [the longest x1 2.5 us: ring_device(): layer_grad = (pair(0) + ups.astype(F32) + downs.astype(F32)).astype(BF16).T]
  transfers between devices with their start and end apart: 2 -> 27, of which waited for: 2 -> 11; matrix products, arithmetic and copies ran while one was open for 30% -> 7% of each run, Pallas kernels for 0% -> 57%
where the time goes in v2:
time: 144 us; the launch traced here: 143 us
  Pallas kernels  82 us (57%)
  waiting for transfers between devices  28.5 us (20%)
  starting transfers between devices  19.3 us (13%)
  other arithmetic  8.1 us (6%)
  local copies, waits for them, and re-layouts  4.71 us (3%)
    pallas_call x4, Pallas kernels, forward(): pl.pallas_call(functools.partial(forward_kernel, k, bool(carry)), grid_sp...  54.3 us
    pallas_call x3, Pallas kernels, partials(): pl.pallas_call(functools.partial(partial_kernel, k), grid_spec=pltpu.Pref...  27.7 us
    ppermute x8, waiting for transfers between devices, send_up(): return lax.ppermute(v, 'row', hop(1))  22.5 us
    ppermute x8, starting transfers between devices, send_up(): return lax.ppermute(v, 'row', hop(1))  14.1 us
    ppermute x8, waiting for transfers between devices, send_down(): return lax.ppermute(v, 'row', hop(-1))  5.98 us
    ppermute x8, starting transfers between devices, send_down(): return lax.ppermute(v, 'row', hop(-1))  3.34 us
  transfers between devices with their start and end apart: 27, of which 11 were waited for; matrix products, arithmetic and copies ran while one was open for 7% of the time, Pallas kernels for 57%

profile of v2, /device:TPU:0, one launch (start us, length us, event | category | flops | bytes accessed | tf_op | source)
XLA Modules:
  0.0 143.5 jit_solution(9986006444072139922)
XLA Ops:
  0.6 3.0 %collective-permute-start = (bf16[192,1536]{1,0:T(8,128)(2,1)}, bf16[192,1536]{1,0:T(8,128)(2,1)}, u32[]{:S(2)}, u32[]{:S(2)}) collective-permute-start(bf16[192,1536]{1,0:T(8,128)(2,1)} %bitcast.67), channel_id=1, source_target_pairs={{2,6},{3,7},{6,10},{7,11},{10,14},{11,15},{14,12},{15,13},{12,8},{... | collective-permute-start | bytes 1769480 | tf_op jit(solution)/shard_map/ppermute | solution.py:124
  7.0 10.2 %shard_map.93 = (bf16[3,192,1536]{2,1,0:T(8,128)(2,1)S(1)}, f32[3,192,1536]{2,1,0:T(8,128)S(1)}, f32[8,128]{1,0:T(8,128)}) custom-call(s32[32]{0:T(128)S(1)} %dynamic-slice_bitcast_fusion.where, bf16[192,1024]{1,0:T(8,128)(2,1)S(1)} %copy.25.mod_t, bf16[1024,24576]{1,0:T(8,128)(2,1)} %w.13), custom_call_target="tpu_custom_call" | custom-call | flops 3623878656 | bytes 18874368 | tf_op jit(solution)/shard_map/pallas_call | solution.py:46
  17.4 1.4 collective-permute-done.1.refs_1_.refs_4_
  18.7 1.6 %collective-permute-start.2 = (bf16[192,1536]{1,0:T(8,128)(2,1)}, bf16[192,1536]{1,0:T(8,128)(2,1)S(1)}, u32[]{:S(2)}, u32[]{:S(2)}) collective-permute-start(bf16[192,1536]{1,0:T(8,128)(2,1)} %collective-permute-done.refs_0_.refs_2_), channel_id=1, source_target_pairs={{2,6},{3,7},{6,10},{7,11},{10,14},{11,15},{14,12},{15,13},{12,8},{... | collective-permute-start | bytes 1769480 | tf_op jit(solution)/shard_map/ppermute | solution.py:124
  20.8 10.2 %shard_map.94 = (bf16[3,192,1536]{2,1,0:T(8,128)(2,1)S(1)}, f32[3,192,1536]{2,1,0:T(8,128)S(1)}, f32[8,128]{1,0:T(8,128)S(1)}) custom-call(s32[32]{0:T(128)S(1)} %dynamic-slice_bitcast_fusion.where, bf16[192,1024]{1,0:T(8,128)(2,1)S(1)} %copy.25.mod_t, bf16[1024,24576]{1,0:T(8,128)(2,1)} %w.13, bf16[192,1536]{1,0:T(8,128)(2,1)} %collective-permute-done.refs_0_.refs_2_, ...), custom_call_target="tpu_custom_call" | custom-call | flops 3623878656 | bytes 18874368 | tf_op jit(solution)/shard_map/pallas_call | solution.py:46
  31.2 1.6 %collective-permute-start.17 = (bf16[192,768]{1,0:T(8,128)(2,1)S(1)}, bf16[192,768]{1,0:T(8,128)(2,1)S(1)}, u32[]{:S(2)}, u32[]{:S(2)}) collective-permute-start(bf16[192,768]{1,0:T(8,128)(2,1)S(1)} %get-tuple-element.69), channel_id=1, source_target_pairs={{2,6},{3,7},{6,10},{7,11},{10,14},{11,15},{14,12},{15,13},{12,8},{... | collective-permute-start | bytes 884744 | tf_op jit(solution)/shard_map/ppermute | solution.py:124
  33.3 1.6 %collective-permute-done.2.refs_0_ = bf16[192,1536]{1,0:T(8,128)(2,1)S(1)} collective-permute-done((bf16[192,1536]{1,0:T(8,128)(2,1)}, bf16[192,1536]{1,0:T(8,128)(2,1)S(1)}, u32[]{:S(2)}, u32[]{:S(2)}) %collective-permute-start.2) | collective-permute-done | bytes 589856 | tf_op jit(solution)/shard_map/ppermute | solution.py:124
  36.2 1.6 %collective-permute-start.4 = (bf16[192,1536]{1,0:T(8,128)(2,1)S(1)}, bf16[192,1536]{1,0:T(8,128)(2,1)S(1)}, u32[]{:S(2)}, u32[]{:S(2)}) collective-permute-start(bf16[192,1536]{1,0:T(8,128)(2,1)S(1)} %collective-permute-done.2.refs_0_), channel_id=1, source_target_pairs={{2,6},{3,7},{6,10},{7,11},{10,14},{11,15},{14,12},{15,13},{12,8},{... | collective-permute-start | bytes 1769480 | tf_op jit(solution)/shard_map/ppermute | solution.py:124
  38.3 3.0 %collective-permute-done.17 = bf16[192,768]{1,0:T(8,128)(2,1)S(1)} collective-permute-done((bf16[192,768]{1,0:T(8,128)(2,1)S(1)}, bf16[192,768]{1,0:T(8,128)(2,1)S(1)}, u32[]{:S(2)}, u32[]{:S(2)}) %collective-permute-start.17) | collective-permute-done | bytes 294944 | tf_op jit(solution)/shard_map/ppermute | solution.py:124
  41.3 1.4 %collective-permute-done.19 = bf16[192,768]{1,0:T(8,128)(2,1)S(1)} collective-permute-done((bf16[192,768]{1,0:T(8,128)(2,1)S(1)}, bf16[192,768]{1,0:T(8,128)(2,1)S(1)}, u32[]{:S(2)}, u32[]{:S(2)}) %collective-permute-start.19) | collective-permute-done | bytes 294944 | tf_op jit(solution)/shard_map/ppermute | solution.py:127
  43.1 1.6 %collective-permute-start.18 = (bf16[192,1536]{1,0:T(8,128)(2,1)S(1)}, bf16[192,1536]{1,0:T(8,128)(2,1)S(1)}, u32[]{:S(2)}, u32[]{:S(2)}) collective-permute-start(bf16[192,1536]{1,0:T(8,128)(2,1)S(1)} %get-tuple-element.65), channel_id=1, source_target_pairs={{2,6},{3,7},{6,10},{7,11},{10,14},{11,15},{14,12},{15,13},{12,8},{... | collective-permute-start | bytes 1769480 | tf_op jit(solution)/shard_map/ppermute | solution.py:124
  44.9 9.0 %collective-permute-done.4.refs_6_.refs_0_ = bf16[192,1536]{1,0:T(8,128)(2,1)S(1)} collective-permute-done((bf16[192,1536]{1,0:T(8,128)(2,1)S(1)}, bf16[192,1536]{1,0:T(8,128)(2,1)S(1)}, u32[]{:S(2)}, u32[]{:S(2)}) %collective-permute-start.4) | collective-permute-done | bytes 589856 | tf_op jit(solution)/shard_map/ppermute | solution.py:124
  55.0 7.3 %shard_map.95 = (bf16[2,192,1536]{2,1,0:T(8,128)(2,1)S(1)}, f32[2,192,1536]{2,1,0:T(8,128)S(1)}, f32[8,128]{1,0:T(8,128)S(1)}) custom-call(s32[32]{0:T(128)S(1)} %dynamic-slice_bitcast_fusion.where, bf16[192,1024]{1,0:T(8,128)(2,1)S(1)} %copy.25.mod_t, bf16[1024,24576]{1,0:T(8,128)(2,1)} %w.13, bf16[192,1536]{1,0:T(8,128)(2,1)S(1)} %collective-permute-done.2.refs_0_, ...), custom_call_target="tpu_custom_call" | custom-call | flops 2415919104 | bytes 12582912 | tf_op jit(solution)/shard_map/pallas_call | solution.py:46
  62.8 3.4 %collective-permute-done.18.refs_8_ = bf16[192,1536]{1,0:T(8,128)(2,1)S(1)} collective-permute-done((bf16[192,1536]{1,0:T(8,128)(2,1)S(1)}, bf16[192,1536]{1,0:T(8,128)(2,1)S(1)}, u32[]{:S(2)}, u32[]{:S(2)}) %collective-permute-start.18) | collective-permute-done | bytes 589856 | tf_op jit(solution)/shard_map/ppermute | solution.py:124
  67.6 1.5 %collective-permute-start.22 = (bf16[192,1536]{1,0:T(8,128)(2,1)S(1)}, bf16[192,1536]{1,0:T(8,128)(2,1)S(1)}, u32[]{:S(2)}, u32[]{:S(2)}) collective-permute-start(bf16[192,1536]{1,0:T(8,128)(2,1)S(1)} %fusion.7), channel_id=1, source_target_pairs={{2,6},{3,7},{6,10},{7,11},{10,14},{11,15},{14,12},{15,13},{12,8},{... | collective-permute-start | bytes 1769480 | tf_op jit(solution)/shard_map/ppermute | solution.py:124
  69.2 19.1 %shard_map.96 = (f32[192,1024]{1,0:T(8,128)S(1)}, bf16[1024,24576]{1,0:T(8,128)(2,1)}, f32[8,128]{1,0:T(8,128)}) custom-call(s32[32]{0:T(128)S(1)} %dynamic-slice_bitcast_fusion.where, bf16[1024,24576]{1,0:T(8,128)(2,1)} %w.13, bf16[1024,192]{1,0:T(8,128)(2,1)S(1)} %fusion.13.mod, bf16[192,1536]{1,0:T(8,128)(2,1)S(1)} %bitcast.70, ...), custom_call_target="tpu_custom_call" | custom-call | flops 7247757312 | bytes 37748736 | tf_op jit(solution)/shard_map/pallas_call | solution.py:92
  88.2 1.6 %collective-permute-start.7 = (bf16[192,768]{1,0:T(8,128)(2,1)S(1)}, bf16[192,768]{1,0:T(8,128)(2,1)S(1)}, u32[]{:S(2)}, u32[]{:S(2)}) collective-permute-start(bf16[192,768]{1,0:T(8,128)(2,1)S(1)} %slice.62), channel_id=1, source_target_pairs={{2,6},{3,7},{6,10},{7,11},{10,14},{11,15},{14,12},{15,13},{12,8},{... | collective-permute-start | bytes 884744 | tf_op jit(solution)/shard_map/ppermute | solution.py:124
  91.5 5.2 %collective-permute-done.7.refs_6_ = bf16[192,768]{1,0:T(8,128)(2,1)S(1)} collective-permute-done((bf16[192,768]{1,0:T(8,128)(2,1)S(1)}, bf16[192,768]{1,0:T(8,128)(2,1)S(1)}, u32[]{:S(2)}, u32[]{:S(2)}) %collective-permute-start.7) | collective-permute-done | bytes 294944 | tf_op jit(solution)/shard_map/ppermute | solution.py:124
  98.7 13.5 %shard_map.97 = (f32[192,1024]{1,0:T(8,128)S(1)}, bf16[1024,24576]{1,0:T(8,128)(2,1)}, f32[8,128]{1,0:T(8,128)}) custom-call(s32[32]{0:T(128)S(1)} %dynamic-slice_bitcast_fusion.where, bf16[1024,24576]{1,0:T(8,128)(2,1)} %w.13, bf16[1024,192]{1,0:T(8,128)(2,1)S(1)} %fusion.13.mod, ...), custom_call_target="tpu_custom_call", output_to_operand_aliasing={{0}: (7, {}), {1}: (8, {})} | custom-call | flops 4831838208 | bytes 25165824 | tf_op jit(solution)/shard_map/pallas_call | solution.py:92
  112.3 1.6 %collective-permute-start.25 = (bf16[192,1536]{1,0:T(8,128)(2,1)}, bf16[192,1536]{1,0:T(8,128)(2,1)}, u32[]{:S(2)}, u32[]{:S(2)}) collective-permute-start(bf16[192,1536]{1,0:T(8,128)(2,1)} %get-tuple-element.62), channel_id=1, source_target_pairs={{2,6},{3,7},{6,10},{7,11},{10,14},{11,15},{14,12},{15,13},{12,8},{... | collective-permute-start | bytes 1769480 | tf_op jit(solution)/shard_map/ppermute | solution.py:124
  115.4 13.5 %shard_map.98 = (f32[192,1024]{1,0:T(8,128)S(1)}, bf16[1024,24576]{1,0:T(8,128)(2,1)}, f32[8,128]{1,0:T(8,128)}) custom-call(s32[32]{0:T(128)S(1)} %dynamic-slice_bitcast_fusion.where, bf16[1024,24576]{1,0:T(8,128)(2,1)} %w.13, bf16[1024,192]{1,0:T(8,128)(2,1)S(1)} %fusion.13.mod, ...), custom_call_target="tpu_custom_call", output_to_operand_aliasing={{0}: (7, {}), {1}: (8, {})} | custom-call | flops 4831838208 | bytes 25165824 | tf_op jit(solution)/shard_map/pallas_call | solution.py:92
  128.9 8.2 %shard_map.99 = (f32[192,1024]{1,0:T(8,128)S(1)}, bf16[1024,24576]{1,0:T(8,128)(2,1)}, f32[8,128]{1,0:T(8,128)}) custom-call(s32[32]{0:T(128)S(1)} %dynamic-slice_bitcast_fusion.where, bf16[1024,24576]{1,0:T(8,128)(2,1)} %w.13, bf16[1024,192]{1,0:T(8,128)(2,1)S(1)} %fusion.13.mod, ...), custom_call_target="tpu_custom_call", output_to_operand_aliasing={{0}: (5, {}), {1}: (6, {})} | custom-call | flops 2415919104 | bytes 12582912 | tf_op jit(solution)/shard_map/pallas_call | solution.py:92
  138.5 1.6 %fusion.18 = bf16[1024,192]{1,0:T(8,128)(2,1)S(1)} fusion(f32[192,1024]{0,1:T(8,128)} %copy.28, bf16[1024,192]{1,0:T(8,128)(2,1)} %copy-done.1, f32[1024]{0:T(1024)S(1)} %copy-done.4), kind=kLoop, calls=%fused_computation.29 | loop fusion | flops 786432 | bytes 1576960 | tf_op jit(solution)/shard_map/transpose | solution.py:234
  141.0 2.5 %fusion.17 = bf16[1536,192]{0,1:T(8,128)(2,1)} fusion(bf16[192,1536]{1,0:T(8,128)(2,1)} %collective-permute-done.26, bf16[192,1536]{1,0:T(8,128)(2,1)} %collective-permute-done.25, f32[2,192,1536]{2,1,0:T(8,128)S(1)} %get-tuple-element.51, bf16[2,192,1536]{2,1,0:T(8,128)(2,1)} %copy-done.2), kind=kLoop, calls=%fused_computation.28 | loop fusion | flops 2064384 | bytes 3538944 | tf_op jit(solution)/shard_map/transpose | solution.py:232
  (67 shorter events, 17.3 us)
Async XLA Ops:
  0.6 16.7 %collective-permute-start = (bf16[192,1536]{1,0:T(8,128)(2,1)}, bf16[192,1536]{1,0:T(8,128)(2,1)}, u32[]{:S(2)}, u32[]{:S(2)}) collective-permute-start(bf16[192,1536]{1,0:T(8,128)(2,1)} %bitcast.67), channel_id=1, source_target_pairs={{2,6},{3,7},{6,10},{7,11},{10,14},{11,15},{14,12},{15,13},{12,8},{... | collective-permute-start | bytes 1769480 | tf_op jit(solution)/shard_map/ppermute | solution.py:124
  3.6 15.1 %collective-permute-start.1 = (bf16[192,1536]{1,0:T(8,128)(2,1)}, bf16[192,1536]{1,0:T(8,128)(2,1)}, u32[]{:S(2)}, u32[]{:S(2)}) collective-permute-start(bf16[192,1536]{1,0:T(8,128)(2,1)} %bitcast.68), channel_id=1, source_target_pairs={{2,0},{3,1},{6,2},{7,3},{10,6},{11,7},{14,10},{15,11},{12,14},{13,... | collective-permute-start | bytes 1769480 | tf_op jit(solution)/shard_map/ppermute | solution.py:127
  18.7 12.3 %collective-permute-start.6 = (bf16[3,192,1536]{2,1,0:T(8,128)(2,1)S(1)}, bf16[3,192,1536]{2,1,0:T(8,128)(2,1)S(1)}, u32[]{:S(2)}, u32[]{:S(2)}) collective-permute-start(bf16[3,192,1536]{2,1,0:T(8,128)(2,1)S(1)} %get-tuple-element.35), channel_id=1, source_target_pairs={{0,1},{1,0},{2,3},{3,2},{4,5},{5,4},{6,7},{7,6},{8,9},{9,8},{10,11... | collective-permute-start | bytes 5308424 | tf_op jit(solution)/shard_map/ppermute | solution.py:130
  18.7 16.2 %collective-permute-start.2 = (bf16[192,1536]{1,0:T(8,128)(2,1)}, bf16[192,1536]{1,0:T(8,128)(2,1)S(1)}, u32[]{:S(2)}, u32[]{:S(2)}) collective-permute-start(bf16[192,1536]{1,0:T(8,128)(2,1)} %collective-permute-done.refs_0_.refs_2_), channel_id=1, source_target_pairs={{2,6},{3,7},{6,10},{7,11},{10,14},{11,15},{14,12},{15,13},{12,8},{... | collective-permute-start | bytes 1769480 | tf_op jit(solution)/shard_map/ppermute | solution.py:124
  20.3 15.9 %collective-permute-start.3 = (bf16[192,1536]{1,0:T(8,128)(2,1)}, bf16[192,1536]{1,0:T(8,128)(2,1)S(1)}, u32[]{:S(2)}, u32[]{:S(2)}) collective-permute-start(bf16[192,1536]{1,0:T(8,128)(2,1)} %collective-permute-done.1.refs_1_.refs_4_), channel_id=1, source_target_pairs={{2,0},{3,1},{6,2},{7,3},{10,6},{11,7},{14,10},{15,11},{12,14},{13,... | collective-permute-start | bytes 1769480 | tf_op jit(solution)/shard_map/ppermute | solution.py:127
  31.0 31.3 %collective-permute-start.21 = (bf16[3,192,1536]{2,1,0:T(8,128)(2,1)S(1)}, bf16[3,192,1536]{2,1,0:T(8,128)(2,1)S(1)}, u32[]{:S(2)}, u32[]{:S(2)}) collective-permute-start(bf16[3,192,1536]{2,1,0:T(8,128)(2,1)S(1)} %get-tuple-element.47), channel_id=1, source_target_pairs={{0,1},{1,0},{2,3},{3,2},{4,5},{5,4},{6,7},{7,6},{8,9},{9,8},{10,11... | collective-permute-start | bytes 5308424 | tf_op jit(solution)/shard_map/ppermute | solution.py:130
  31.2 10.0 %collective-permute-start.17 = (bf16[192,768]{1,0:T(8,128)(2,1)S(1)}, bf16[192,768]{1,0:T(8,128)(2,1)S(1)}, u32[]{:S(2)}, u32[]{:S(2)}) collective-permute-start(bf16[192,768]{1,0:T(8,128)(2,1)S(1)} %get-tuple-element.69), channel_id=1, source_target_pairs={{2,6},{3,7},{6,10},{7,11},{10,14},{11,15},{14,12},{15,13},{12,8},{... | collective-permute-start | bytes 884744 | tf_op jit(solution)/shard_map/ppermute | solution.py:124
  36.2 17.7 %collective-permute-start.4 = (bf16[192,1536]{1,0:T(8,128)(2,1)S(1)}, bf16[192,1536]{1,0:T(8,128)(2,1)S(1)}, u32[]{:S(2)}, u32[]{:S(2)}) collective-permute-start(bf16[192,1536]{1,0:T(8,128)(2,1)S(1)} %collective-permute-done.2.refs_0_), channel_id=1, source_target_pairs={{2,6},{3,7},{6,10},{7,11},{10,14},{11,15},{14,12},{15,13},{12,8},{... | collective-permute-start | bytes 1769480 | tf_op jit(solution)/shard_map/ppermute | solution.py:124
  37.8 17.1 %collective-permute-start.5 = (bf16[192,1536]{1,0:T(8,128)(2,1)S(1)}, bf16[192,1536]{1,0:T(8,128)(2,1)S(1)}, u32[]{:S(2)}, u32[]{:S(2)}) collective-permute-start(bf16[192,1536]{1,0:T(8,128)(2,1)S(1)} %collective-permute-done.3.refs_1_.refs_2_), channel_id=1, source_target_pairs={{2,0},{3,1},{6,2},{7,3},{10,6},{11,7},{14,10},{15,11},{12,14},{13,... | collective-permute-start | bytes 1769480 | tf_op jit(solution)/shard_map/ppermute | solution.py:127
  43.1 23.2 %collective-permute-start.18 = (bf16[192,1536]{1,0:T(8,128)(2,1)S(1)}, bf16[192,1536]{1,0:T(8,128)(2,1)S(1)}, u32[]{:S(2)}, u32[]{:S(2)}) collective-permute-start(bf16[192,1536]{1,0:T(8,128)(2,1)S(1)} %get-tuple-element.65), channel_id=1, source_target_pairs={{2,6},{3,7},{6,10},{7,11},{10,14},{11,15},{14,12},{15,13},{12,8},{... | collective-permute-start | bytes 1769480 | tf_op jit(solution)/shard_map/ppermute | solution.py:124
  44.7 21.8 %collective-permute-start.14 = (bf16[192,1536]{1,0:T(8,128)(2,1)S(1)}, bf16[192,1536]{1,0:T(8,128)(2,1)S(1)}, u32[]{:S(2)}, u32[]{:S(2)}) collective-permute-start(bf16[192,1536]{1,0:T(8,128)(2,1)S(1)} %bitcast.69), channel_id=1, source_target_pairs={{0,1},{1,0},{2,3},{3,2},{4,5},{5,4},{6,7},{7,6},{8,9},{9,8},{10,11... | collective-permute-start | bytes 1769480 | tf_op jit(solution)/shard_map/ppermute | solution.py:130
  53.9 13.2 %collective-permute-start.15 = (bf16[192,1536]{1,0:T(8,128)(2,1)}, bf16[192,1536]{1,0:T(8,128)(2,1)S(1)}, u32[]{:S(2)}, u32[]{:S(2)}) collective-permute-start(bf16[192,1536]{1,0:T(8,128)(2,1)} %collective-permute-done.refs_0_.refs_2_), channel_id=1, source_target_pairs={{0,1},{1,0},{2,3},{3,2},{4,5},{5,4},{6,7},{7,6},{8,9},{9,8},{10,11... | collective-permute-start | bytes 1769480 | tf_op jit(solution)/shard_map/ppermute | solution.py:130
  54.9 12.7 %collective-permute-start.16 = (bf16[192,1536]{1,0:T(8,128)(2,1)}, bf16[192,1536]{1,0:T(8,128)(2,1)S(1)}, u32[]{:S(2)}, u32[]{:S(2)}) collective-permute-start(bf16[192,1536]{1,0:T(8,128)(2,1)} %collective-permute-done.1.refs_1_.refs_4_), channel_id=1, source_target_pairs={{0,1},{1,0},{2,3},{3,2},{4,5},{5,4},{6,7},{7,6},{8,9},{9,8},{10,11... | collective-permute-start | bytes 1769480 | tf_op jit(solution)/shard_map/ppermute | solution.py:130
  62.3 35.8 %collective-permute-start.12 = (bf16[192,1536]{1,0:T(8,128)(2,1)S(1)}, bf16[192,1536]{1,0:T(8,128)(2,1)S(1)}, u32[]{:S(2)}, u32[]{:S(2)}) collective-permute-start(bf16[192,1536]{1,0:T(8,128)(2,1)S(1)} %collective-permute-done.2.refs_0_), channel_id=1, source_target_pairs={{0,1},{1,0},{2,3},{3,2},{4,5},{5,4},{6,7},{7,6},{8,9},{9,8},{10,11... | collective-permute-start | bytes 1769480 | tf_op jit(solution)/shard_map/ppermute | solution.py:130
  66.3 32.4 %collective-permute-start.13 = (bf16[192,1536]{1,0:T(8,128)(2,1)S(1)}, bf16[192,1536]{1,0:T(8,128)(2,1)S(1)}, u32[]{:S(2)}, u32[]{:S(2)}) collective-permute-start(bf16[192,1536]{1,0:T(8,128)(2,1)S(1)} %collective-permute-done.3.refs_1_.refs_2_), channel_id=1, source_target_pairs={{0,1},{1,0},{2,3},{3,2},{4,5},{5,4},{6,7},{7,6},{8,9},{9,8},{10,11... | collective-permute-start | bytes 1769480 | tf_op jit(solution)/shard_map/ppermute | solution.py:130
  66.6 45.7 %collective-permute-start.24 = (bf16[2,192,1536]{2,1,0:T(8,128)(2,1)S(1)}, bf16[2,192,1536]{2,1,0:T(8,128)(2,1)S(1)}, u32[]{:S(2)}, u32[]{:S(2)}) collective-permute-start(bf16[2,192,1536]{2,1,0:T(8,128)(2,1)S(1)} %get-tuple-element.52), channel_id=1, source_target_pairs={{0,1},{1,0},{2,3},{3,2},{4,5},{5,4},{6,7},{7,6},{8,9},{9,8},{10,11... | collective-permute-start | bytes 3538952 | tf_op jit(solution)/shard_map/ppermute | solution.py:130
  67.1 21.1 %collective-permute-start.20 = (bf16[192,1536]{1,0:T(8,128)(2,1)S(1)}, bf16[192,1536]{1,0:T(8,128)(2,1)S(1)}, u32[]{:S(2)}, u32[]{:S(2)}) collective-permute-start(bf16[192,1536]{1,0:T(8,128)(2,1)S(1)} %get-tuple-element.64), channel_id=1, source_target_pairs={{2,0},{3,1},{6,2},{7,3},{10,6},{11,7},{14,10},{15,11},{12,14},{13,... | collective-permute-start | bytes 1769480 | tf_op jit(solution)/shard_map/ppermute | solution.py:127
  67.6 22.2 %collective-permute-start.22 = (bf16[192,1536]{1,0:T(8,128)(2,1)S(1)}, bf16[192,1536]{1,0:T(8,128)(2,1)S(1)}, u32[]{:S(2)}, u32[]{:S(2)}) collective-permute-start(bf16[192,1536]{1,0:T(8,128)(2,1)S(1)} %fusion.7), channel_id=1, source_target_pairs={{2,6},{3,7},{6,10},{7,11},{10,14},{11,15},{14,12},{15,13},{12,8},{... | collective-permute-start | bytes 1769480 | tf_op jit(solution)/shard_map/ppermute | solution.py:124
  96.7 17.1 %collective-permute-start.23 = (bf16[192,1536]{1,0:T(8,128)(2,1)S(1)}, bf16[192,1536]{1,0:T(8,128)(2,1)S(1)}, u32[]{:S(2)}, u32[]{:S(2)}) collective-permute-start(bf16[192,1536]{1,0:T(8,128)(2,1)S(1)} %get-tuple-element.63), channel_id=1, source_target_pairs={{2,0},{3,1},{6,2},{7,3},{10,6},{11,7},{14,10},{15,11},{12,14},{13,... | collective-permute-start | bytes 1769480 | tf_op jit(solution)/shard_map/ppermute | solution.py:127
  98.0 17.3 %collective-permute-start.10 = (bf16[192,1536]{1,0:T(8,128)(2,1)S(1)}, bf16[192,1536]{1,0:T(8,128)(2,1)S(1)}, u32[]{:S(2)}, u32[]{:S(2)}) collective-permute-start(bf16[192,1536]{1,0:T(8,128)(2,1)S(1)} %collective-permute-done.4.refs_6_.refs_0_), channel_id=1, source_target_pairs={{0,1},{1,0},{2,3},{3,2},{4,5},{5,4},{6,7},{7,6},{8,9},{9,8},{10,11... | collective-permute-start | bytes 1769480 | tf_op jit(solution)/shard_map/ppermute | solution.py:130
  98.1 17.3 %collective-permute-start.11 = (bf16[192,1536]{1,0:T(8,128)(2,1)S(1)}, bf16[192,1536]{1,0:T(8,128)(2,1)S(1)}, u32[]{:S(2)}, u32[]{:S(2)}) collective-permute-start(bf16[192,1536]{1,0:T(8,128)(2,1)S(1)} %collective-permute-done.5.refs_7_.refs_2_), channel_id=1, source_target_pairs={{0,1},{1,0},{2,3},{3,2},{4,5},{5,4},{6,7},{7,6},{8,9},{9,8},{10,11... | collective-permute-start | bytes 1769480 | tf_op jit(solution)/shard_map/ppermute | solution.py:130
  98.7 30.2 %collective-permute-start.9 = (bf16[192,1536]{1,0:T(8,128)(2,1)S(1)}, bf16[192,1536]{1,0:T(8,128)(2,1)S(1)}, u32[]{:S(2)}, u32[]{:S(2)}) collective-permute-start(bf16[192,1536]{1,0:T(8,128)(2,1)S(1)} %constant_dynamic-update-slice_fusion.refs_0_), channel_id=1, source_target_pairs={{0,1},{1,0},{2,3},{3,2},{4,5},{5,4},{6,7},{7,6},{8,9},{9,8},{10,11... | collective-permute-start | bytes 1769480 | tf_op jit(solution)/shard_map/ppermute | solution.py:130
  112.3 28.7 %collective-permute-start.25 = (bf16[192,1536]{1,0:T(8,128)(2,1)}, bf16[192,1536]{1,0:T(8,128)(2,1)}, u32[]{:S(2)}, u32[]{:S(2)}) collective-permute-start(bf16[192,1536]{1,0:T(8,128)(2,1)} %get-tuple-element.62), channel_id=1, source_target_pairs={{2,6},{3,7},{6,10},{7,11},{10,14},{11,15},{14,12},{15,13},{12,8},{... | collective-permute-start | bytes 1769480 | tf_op jit(solution)/shard_map/ppermute | solution.py:124
  114.9 26.0 %collective-permute-start.26 = (bf16[192,1536]{1,0:T(8,128)(2,1)}, bf16[192,1536]{1,0:T(8,128)(2,1)}, u32[]{:S(2)}, u32[]{:S(2)}) collective-permute-start(bf16[192,1536]{1,0:T(8,128)(2,1)} %fusion.2), channel_id=1, source_target_pairs={{2,0},{3,1},{6,2},{7,3},{10,6},{11,7},{14,10},{15,11},{12,14},{13,... | collective-permute-start | bytes 1769480 | tf_op jit(solution)/shard_map/ppermute | solution.py:127
  (8 other events, 97.1 us)
